TPU v7x, 32 devices: a whole 2x2x4 slice. The times are simulated.
32 devices in a mesh: dom: 32 (over z, y, x, core).
Axes of the slice: x: 2, y: 2, z: 4, core: 2. Of those that a mesh axis runs over, the one named last changes fastest.
Arguments:
- right_side: float32 [64, 4096], P(None, 'dom'), may hold values from -8 to 8
- sigma: float32 [64, 4096], P(None, 'dom'), may hold values from 0.5 to 2
- reluctivity: float32 [64, 4096], P(None, 'dom'), may hold values from 0.2 to 5
- curl_blocks: float32 [6, 64, 64, 4096], P(None, None, None, 'dom'), may hold values from -0.3125 to 0.3125
- pattern: int32 [6, 4096], P(None, 'dom'), may hold values from 0 to 191
- cond_weight: float32 [64, 16384], P(None, 'dom'), may hold values from -0.25 to 0.25
- cond_block: int32 [16384], P('dom'), may hold values from 0 to 127
- cond_coil: int32 [16384, 1], P('dom'), may hold values from 0 to 83; in each aligned block of 512 rows (0 to 511, 512 to 1023, ...) at most 16 rows name the same one
- coil_phase: int32 [84], replicated, may hold values from 0 to 3
- coil_resistance: float32 [84], replicated, may hold values from 0.5 to 2
- switch_state: int32 [3], replicated, may hold values from 0 to 1
Outputs:
- solution_field: float32 [64, 4096], P(None, 'dom')
- residual: float32 [64, 4096], P(None, 'dom')
Inputs may be any that keep to these rules, and one draw needn't show every extreme that they name: `cond_coil`: no coil is named by more than 16 of one partition's 512 conductor rows, a bound that some block reaches.
All inputs are finite; a program needn't handle non-finite values.
Results may differ from a plain program's by a relative error of at most 0.00055.
Values sent between devices are 32-bit elements; how exact they have to be, the bound alone decides.
A program may use at most 64 MiB of HBM per device.

v0:
```python
import jax
import jax.numpy as jnp
from jax import lax
from jax.sharding import PartitionSpec as P

ITERS = 3


link_scale = 16.0


def extended_2(block, sides, width):
    for axis, dim in sides:
        count = lax.axis_size(axis)
        forward = [(i, i + 1) for i in range(count - 1)]
        backward = [(target, source) for source, target in forward]
        low = lax.ppermute(
            lax.slice_in_dim(block, block.shape[dim] - width, None, axis=dim), axis, forward
        )
        high = lax.ppermute(lax.slice_in_dim(block, 0, width, axis=dim), axis, backward)
        block = jnp.concatenate([low, block, high], axis=dim)
    return block


def shifted(array, axis, by):
    devices = lax.axis_size(axis)
    pairs = [(i, i + by) for i in range(devices) if 0 <= i + by < devices]
    return lax.ppermute(array, axis, pairs)


def body(
    right_side,
    sigma,
    reluctivity,
    curl_blocks,
    pattern,
    cond_weight,
    cond_block,
    cond_coil,
    coil_phase,
    coil_resistance,
    switch_state,
):
    block_count = right_side.shape[1]
    halo_width = block_count // 4
    coil_rows = cond_coil[:, 0]
    coil_count = coil_resistance.shape[0]
    highest = lax.Precision.HIGHEST
    coil_iota = jnp.arange(coil_count, dtype=jnp.int32)
    row_onehot = (coil_rows[:, None] == coil_iota[None, :]).astype(jnp.float32)
    switch_float = switch_state.astype(jnp.float32)
    phase_volts = jnp.concatenate(
        [switch_float - jnp.mean(switch_float), jnp.zeros((1,), jnp.float32)]
    )
    phase_iota = jnp.arange(phase_volts.shape[0], dtype=jnp.int32)
    phase_onehot = (coil_phase[:, None] == phase_iota[None, :]).astype(jnp.float32)
    coil_volts = link_scale * jnp.dot(phase_onehot, phase_volts, precision=highest)
    row_source = jnp.dot(row_onehot, coil_volts / coil_resistance, precision=highest)
    rhs = right_side + jnp.zeros_like(right_side).at[:, cond_block].add(
        cond_weight * row_source[None, :]
    )

    def squares(vector):
        return lax.psum(jnp.sum(vector * vector), "dom")

    solution_field = jnp.zeros_like(rhs)
    residual = rhs
    direction = rhs
    norm_now = squares(residual)
    for turn_index in range(ITERS):
        extended = extended_2(direction, (("dom", 1),), halo_width)
        picked = jnp.take(extended, pattern, axis=1)
        face_flux = jnp.einsum("kabn,bkn->an", curl_blocks, picked, precision=highest)
        back_terms = jnp.einsum(
            "kabn,an->bkn", curl_blocks, reluctivity * face_flux, precision=highest
        )
        spread = jnp.zeros_like(extended).at[:, pattern].add(back_terms)
        centre = spread[:, halo_width : halo_width + block_count]
        from_next = shifted(spread[:, :halo_width], "dom", -1)
        from_prev = shifted(spread[:, halo_width + block_count :], "dom", 1)
        centre = centre.at[:, block_count - halo_width :].add(from_next)
        centre = centre.at[:, :halo_width].add(from_prev)
        picked_rows = jnp.take(direction, cond_block, axis=1)
        partial_link = jnp.dot(
            jnp.sum(cond_weight * picked_rows, axis=0), row_onehot, precision=highest
        )
        linkage = lax.psum(partial_link, "dom")
        row_current = jnp.dot(row_onehot, linkage / coil_resistance, precision=highest)
        coupled = (
            jnp.zeros_like(direction).at[:, cond_block].add(cond_weight * row_current[None, :])
        )
        image = sigma * direction + centre + coupled
        alpha = norm_now / lax.psum(jnp.sum(direction * image), "dom")
        solution_field = solution_field + alpha * direction
        residual = residual - alpha * image
        norm_next = squares(residual)
        direction = residual + norm_next / norm_now * direction
        norm_now = norm_next
    return (solution_field, residual)


def solution(mesh):
    return jax.shard_map(
        body,
        mesh=mesh,
        in_specs=(
            P(None, "dom"),
            P(None, "dom"),
            P(None, "dom"),
            P(None, None, None, "dom"),
            P(None, "dom"),
            P(None, "dom"),
            P("dom"),
            P("dom", None),
            P(),
            P(),
            P(),
        ),
        out_specs=(P(None, "dom"), P(None, "dom")),
        check_vma=False,
    )
```

profile of v0, /device:TPU:0, one launch (start us, length us, event | category | flops | bytes accessed | tf_op | source)
XLA Modules:
  0.0 485.0 jit_solution(3989023422105243589)
XLA Ops:
  7.7 3.3 scatter_fusion
  20.1 44.7 %psum.64 = f32[84]{0:T(128)S(1)} all-reduce(f32[84]{0:T(128)S(1)} %convolution_bitcast_fusion.2), channel_id=1, replica_groups=mesh['dom'=32] {'dom'}, use_global_device_ids=true, to_apply=%region_7.0 | all-reduce | flops 84 | bytes 672 | tf_op jit(solution)/shard_map/psum | solution.py:87
  67.8 6.6 %multiply_reduce_fusion.5 = f32[128,64]{0,1:T(8,128)S(1)} fusion(f32[6,64,64,128]{3,2,1,0:T(8,128)} %param.30, f32[128,64,6]{0,1,2:T(8,128)S(1)} %copy.68), kind=kLoop, calls=%fused_computation.18 | loop fusion | flops 6283264 | bytes 12812288 | tf_op jit(solution)/shard_map/kabn,bkn->an/dot_general | solution.py:73
  77.7 6.1 %scatter_custom_fusion.1 = f32[64,192]{0,1:T(8,128)S(1)} fusion(s32[768]{0:T(1024)S(1)} %fusion.33, f32[768,64]{1,0:T(8,128)S(1)} %bitcast.123, f32[]{:T(128)} %constant.166.clone.1), kind=kCustom, calls=%fused_computation.73 | custom fusion | flops 49152 | bytes 49156 | tf_op jit(solution)/shard_map/scatter-add | solution.py:77
  86.0 3.0 collective-permute-start.3
  90.6 3.6 scatter_fusion.1
  94.9 44.2 %all-reduce = (f32[]{:T(128)}, f32[]{:T(128)}) all-reduce(f32[]{:T(128)} %get-tuple-element.79, f32[]{:T(128)} %get-tuple-element.78), channel_id=1, replica_groups=mesh['dom'=32] {'dom'}, use_global_device_ids=true, to_apply=%region_3.0 | all-reduce | flops 2 | bytes 16 | tf_op jit(solution)/shard_map/psum | solution.py:64
  141.0 39.7 %psum.66 = f32[]{:T(128)} all-reduce(f32[]{:T(128)} %multiply_reduce_fusion.9), channel_id=1, replica_groups=mesh['dom'=32] {'dom'}, use_global_device_ids=true, to_apply=%region_12.15 | all-reduce | flops 1 | bytes 8 | tf_op jit(solution)/shard_map/psum | solution.py:64
  186.2 43.8 %psum.67 = f32[84]{0:T(128)S(1)} all-reduce(f32[84]{0:T(128)S(1)} %convolution_bitcast_fusion.1), channel_id=1, replica_groups=mesh['dom'=32] {'dom'}, use_global_device_ids=true, to_apply=%region_15.18 | all-reduce | flops 84 | bytes 672 | tf_op jit(solution)/shard_map/psum | solution.py:87
  232.2 6.3 %multiply_reduce_fusion.3 = f32[128,64]{0,1:T(8,128)S(1)} fusion(f32[6,64,64,128]{3,2,1,0:T(8,128)} %param.30, f32[128,64,6]{0,1,2:T(8,128)S(1)} %copy.70), kind=kLoop, calls=%fused_computation.16 | loop fusion | flops 6283264 | bytes 12812288 | tf_op jit(solution)/shard_map/kabn,bkn->an/dot_general | solution.py:73
  238.6 6.2 %multiply_reduce_fusion.2 = f32[128,6,64]{0,2,1:T(8,128)S(1)} fusion(f32[6,64,64,128]{3,2,1,0:T(8,128)} %param.30, f32[128,64]{0,1:T(8,128)S(1)} %fusion.24), kind=kLoop, calls=%fused_computation.15 | loop fusion | flops 6242304 | bytes 12812288
  245.0 6.1 %scatter_custom_fusion.3 = f32[64,192]{0,1:T(8,128)S(1)} fusion(s32[768]{0:T(1024)S(1)} %fusion.33, f32[768,64]{1,0:T(8,128)S(1)} %bitcast.124, f32[]{:T(128)} %constant.166.clone.1), kind=kCustom, calls=%fused_computation.71 | custom fusion | flops 49152 | bytes 49156 | tf_op jit(solution)/shard_map/scatter-add | solution.py:77
  251.0 12.3 %collective-permute-start.6 = (f32[64,32]{0,1:T(8,128)S(1)}, f32[64,32]{0,1:T(8,128)S(1)}, u32[]{:S(2)}, u32[]{:S(2)}) collective-permute-start(f32[64,32]{0,1:T(8,128)S(1)} %get-tuple-element.87), channel_id=1, source_target_pairs={{1,0},{2,1},{3,2},{4,3},{5,4},{6,5},{7,6},{8,7},{9,8},{10,9},{11,1... | collective-permute-start | bytes 24584 | tf_op jit(solution)/shard_map/ppermute | solution.py:28
  263.5 3.0 collective-permute-start.7
  268.1 3.3 scatter_fusion.2
  272.1 43.9 %psum.68 = f32[]{:T(128)} all-reduce(f32[]{:T(128)} %multiply_reduce_fusion.8), channel_id=1, replica_groups=mesh['dom'=32] {'dom'}, use_global_device_ids=true, to_apply=%region_18.21 | all-reduce | flops 1 | bytes 8 | tf_op jit(solution)/shard_map/psum | solution.py:93
  318.1 39.9 %psum.69 = f32[]{:T(128)} all-reduce(f32[]{:T(128)} %get-tuple-element.82), channel_id=1, replica_groups=mesh['dom'=32] {'dom'}, use_global_device_ids=true, to_apply=%region_20.23 | all-reduce | flops 1 | bytes 8 | tf_op jit(solution)/shard_map/psum | solution.py:64
  363.4 43.8 %psum.70 = f32[84]{0:T(128)S(1)} all-reduce(f32[84]{0:T(128)S(1)} %convolution_bitcast_fusion), channel_id=1, replica_groups=mesh['dom'=32] {'dom'}, use_global_device_ids=true, to_apply=%region_23.26 | all-reduce | flops 84 | bytes 672 | tf_op jit(solution)/shard_map/psum | solution.py:87
  409.5 6.3 %multiply_reduce_fusion.1 = f32[128,64]{0,1:T(8,128)S(1)} fusion(f32[6,64,64,128]{3,2,1,0:T(8,128)} %param.30, f32[128,64,6]{0,1,2:T(8,128)S(1)} %copy.72), kind=kLoop, calls=%fused_computation.14 | loop fusion | flops 6283264 | bytes 12812288 | tf_op jit(solution)/shard_map/kabn,bkn->an/dot_general | solution.py:73
  415.8 6.2 %multiply_reduce_fusion = f32[128,6,64]{0,2,1:T(8,128)S(1)} fusion(f32[6,64,64,128]{3,2,1,0:T(8,128)} %param.30, f32[128,64]{0,1:T(8,128)S(1)} %fusion.23), kind=kLoop, calls=%fused_computation.13 | loop fusion | flops 6242304 | bytes 12812288
  422.2 6.1 %scatter_custom_fusion.5 = f32[64,192]{0,1:T(8,128)S(1)} fusion(s32[768]{0:T(1024)S(1)} %fusion.33, f32[768,64]{1,0:T(8,128)S(1)} %bitcast.122, f32[]{:T(128)} %constant.166.clone.1), kind=kCustom, calls=%fused_computation.69 | custom fusion | flops 49152 | bytes 49156 | tf_op jit(solution)/shard_map/scatter-add | solution.py:77
  429.7 3.0 collective-permute-start.11
  434.3 3.3 scatter_fusion.3
  438.2 43.9 %psum.71 = f32[]{:T(128)} all-reduce(f32[]{:T(128)} %multiply_reduce_fusion.6), channel_id=1, replica_groups=mesh['dom'=32] {'dom'}, use_global_device_ids=true, to_apply=%region_26.29 | all-reduce | flops 1 | bytes 8 | tf_op jit(solution)/shard_map/psum | solution.py:93
  (113 shorter events, 47.7 us)
Async XLA Ops:
  0.6 73.7 %copy-start.2 = (f32[64,128]{1,0:T(8,128)S(1)}, f32[64,128]{1,0:T(8,128)}, u32[]{:S(2)}) copy-start(f32[64,128]{1,0:T(8,128)} %param.29) | copy-start | bytes 98308
  11.1 54.7 %collective-permute-start = (f32[64,32]{0,1:T(8,128)S(1)}, f32[64,32]{0,1:T(8,128)S(1)}, u32[]{:S(2)}, u32[]{:S(2)}) collective-permute-start(f32[64,32]{0,1:T(8,128)S(1)} %get-tuple-element.94), channel_id=1, source_target_pairs={{0,1},{1,2},{2,3},{3,4},{4,5},{5,6},{6,7},{7,8},{8,9},{9,10},{10,1... | collective-permute-start | bytes 24584 | tf_op jit(solution)/shard_map/ppermute | solution.py:17
  13.5 52.3 %collective-permute-start.1 = (f32[64,32]{0,1:T(8,128)S(1)}, f32[64,32]{0,1:T(8,128)S(1)}, u32[]{:S(2)}, u32[]{:S(2)}) collective-permute-start(f32[64,32]{0,1:T(8,128)S(1)} %get-tuple-element.95), channel_id=1, source_target_pairs={{1,0},{2,1},{3,2},{4,3},{5,4},{6,5},{7,6},{8,7},{9,8},{10,9},{11,1... | collective-permute-start | bytes 24584 | tf_op jit(solution)/shard_map/ppermute | solution.py:20
  67.7 8.2 %copy-start = (f32[6,64,64,128]{3,2,1,0:T(8,128)S(1)}, f32[6,64,64,128]{3,2,1,0:T(8,128)}, u32[]{:S(2)}) copy-start(f32[6,64,64,128]{3,2,1,0:T(8,128)} %param.30) | copy-start | bytes 37748740
  67.7 17.4 %copy-start.1 = (f32[64,512]{1,0:T(8,128)S(1)}, f32[64,512]{1,0:T(8,128)}, u32[]{:S(2)}) copy-start(f32[64,512]{1,0:T(8,128)} %param.32) | copy-start | bytes 393220
  67.8 17.4 %copy-start.3 = (f32[64,128]{1,0:T(8,128)S(1)}, f32[64,128]{1,0:T(8,128)}, u32[]{:S(2)}) copy-start(f32[64,128]{1,0:T(8,128)} %param.28) | copy-start | bytes 98308
  74.3 111.5 %copy-start.4 = (s32[512,1]{0,1:T(1,128)S(1)}, s32[512,1]{0,1:T(1,128)}, u32[]{:S(2)}) copy-start(s32[512,1]{0,1:T(1,128)} %param.34) | copy-start | bytes 6148
  74.4 155.6 %copy-start.5 = (f32[84]{0:T(128)S(1)}, f32[84]{0:T(128)}, u32[]{:S(2)}) copy-start(f32[84]{0:T(128)} %param.36) | copy-start | bytes 1012
  83.8 5.3 %collective-permute-start.2 = (f32[64,32]{0,1:T(8,128)S(1)}, f32[64,32]{0,1:T(8,128)S(1)}, u32[]{:S(2)}, u32[]{:S(2)}) collective-permute-start(f32[64,32]{0,1:T(8,128)S(1)} %get-tuple-element.89), channel_id=1, source_target_pairs={{1,0},{2,1},{3,2},{4,3},{5,4},{6,5},{7,6},{8,7},{9,8},{10,9},{11,1... | collective-permute-start | bytes 24584 | tf_op jit(solution)/shard_map/ppermute | solution.py:28
  86.0 3.8 collective-permute-start.3
  183.1 47.2 %collective-permute-start.4 = (f32[64,32]{0,1:T(8,128)S(1)}, f32[64,32]{0,1:T(8,128)S(1)}, u32[]{:S(2)}, u32[]{:S(2)}) collective-permute-start(f32[64,32]{0,1:T(8,128)S(1)} %get-tuple-element.92), channel_id=1, source_target_pairs={{0,1},{1,2},{2,3},{3,4},{4,5},{5,6},{6,7},{7,8},{8,9},{9,10},{10,1... | collective-permute-start | bytes 24584 | tf_op jit(solution)/shard_map/ppermute | solution.py:17
  184.4 46.0 %collective-permute-start.5 = (f32[64,32]{0,1:T(8,128)S(1)}, f32[64,32]{0,1:T(8,128)S(1)}, u32[]{:S(2)}, u32[]{:S(2)}) collective-permute-start(f32[64,32]{0,1:T(8,128)S(1)} %get-tuple-element.93), channel_id=1, source_target_pairs={{1,0},{2,1},{3,2},{4,3},{5,4},{6,5},{7,6},{8,7},{9,8},{10,9},{11,1... | collective-permute-start | bytes 24584 | tf_op jit(solution)/shard_map/ppermute | solution.py:20
  251.0 15.5 %collective-permute-start.6 = (f32[64,32]{0,1:T(8,128)S(1)}, f32[64,32]{0,1:T(8,128)S(1)}, u32[]{:S(2)}, u32[]{:S(2)}) collective-permute-start(f32[64,32]{0,1:T(8,128)S(1)} %get-tuple-element.87), channel_id=1, source_target_pairs={{1,0},{2,1},{3,2},{4,3},{5,4},{6,5},{7,6},{8,7},{9,8},{10,9},{11,1... | collective-permute-start | bytes 24584 | tf_op jit(solution)/shard_map/ppermute | solution.py:28
  263.5 3.9 collective-permute-start.7
  360.3 47.2 %collective-permute-start.8 = (f32[64,32]{0,1:T(8,128)S(1)}, f32[64,32]{0,1:T(8,128)S(1)}, u32[]{:S(2)}, u32[]{:S(2)}) collective-permute-start(f32[64,32]{0,1:T(8,128)S(1)} %get-tuple-element.90), channel_id=1, source_target_pairs={{0,1},{1,2},{2,3},{3,4},{4,5},{5,6},{6,7},{7,8},{8,9},{9,10},{10,1... | collective-permute-start | bytes 24584 | tf_op jit(solution)/shard_map/ppermute | solution.py:17
  361.6 45.9 %collective-permute-start.9 = (f32[64,32]{0,1:T(8,128)S(1)}, f32[64,32]{0,1:T(8,128)S(1)}, u32[]{:S(2)}, u32[]{:S(2)}) collective-permute-start(f32[64,32]{0,1:T(8,128)S(1)} %get-tuple-element.91), channel_id=1, source_target_pairs={{1,0},{2,1},{3,2},{4,3},{5,4},{6,5},{7,6},{8,7},{9,8},{10,9},{11,1... | collective-permute-start | bytes 24584 | tf_op jit(solution)/shard_map/ppermute | solution.py:20
  428.3 4.5 collective-permute-start.10
  429.7 3.9 collective-permute-start.11
where the time goes:
time: 490 us; the launch traced here: 485 us
  blocking collectives  344 us (70%)
  other arithmetic  78 us (16%)
  starting transfers between devices  32.8 us (7%)
  local copies, waits for them, and re-layouts  14.2 us (3%)
  between operations  8.6 us (2%)
  matrix products  5.01 us (1%)
    psum x3, blocking collectives, body(): linkage = lax.psum(partial_link, 'dom')  132 us
    psum x3, blocking collectives, squares(): return lax.psum(jnp.sum(vector * vector), 'dom')  124 us
    psum x2, blocking collectives, body(): alpha = norm_now / lax.psum(jnp.sum(direction * image), 'dom')  87.8 us
    ppermute x6, starting transfers between devices, shifted(): return lax.ppermute(array, axis, pairs)  24 us
    dot_general x3, other arithmetic, body(): jnp.einsum('kabn,bkn->an', curl_blocks, picked, precision=highest)  19.2 us
    scatter-add x3, other arithmetic, body(): spread = jnp.zeros_like(extended).at[:, pattern].add(back_terms)  18.2 us
    unnamed x9, other arithmetic  14.6 us
    scatter-add x3, other arithmetic, body(): jnp.zeros_like(direction).at[:, cond_block]  10.3 us
  transfers between devices with their start and end apart: 12, of which 3 were waited for; matrix products, arithmetic and copies ran while one was open for 2% of the time, Pallas kernels for 0%

commit v1 on v0

v1 whole, which is shorter than its diff:
```python
import functools

import jax
import jax.numpy as jnp
from jax import lax
from jax.experimental import pallas as pl
from jax.experimental.pallas import tpu as pltpu
from jax.sharding import PartitionSpec as P

ITERS = 3
LINK_SCALE = 16.0
LANES = 128
RR_ROW = 126
RAR_ROW = 127
MESH = pl.DeviceIdType.MESH
F32 = jnp.float32
BF16 = jnp.bfloat16


def split2(x):
    high = x.astype(BF16)
    low = (x - high.astype(F32)).astype(BF16)
    return jnp.concatenate([high, low], axis=0)


def pick(x, onehot):
    rows = x.shape[0]
    both = jnp.dot(split2(x), onehot, preferred_element_type=F32)
    return both[:rows] + both[rows:]


def place(x, onehot):
    rows = x.shape[0]
    both = lax.dot_general(
        split2(x), onehot, (((1,), (1,)), ((), ())), preferred_element_type=F32
    )
    return both[:rows] + both[rows:]


def onehot_of(index_row, height):
    iota = lax.broadcasted_iota(jnp.int32, (height, index_row.shape[1]), 0)
    return jnp.where(iota == index_row, 1.0, 0.0).astype(BF16)


def row_iota(width):
    return lax.broadcasted_iota(jnp.int32, (1, width), 1)


def kernel(
    n,
    rs_ref,
    sigma_ref,
    nu_ref,
    curl_hbm,
    pat_ref,
    cw_ref,
    meta_ref,
    x_ref,
    r_ref,
    curl,
    oh_pat,
    oh_blk,
    oh_nbr,
    oh_coil,
    picked,
    back,
    dacc,
    cw_nbr,
    meta_nbr,
    msg,
    msg_in,
    row,
    row_in,
    curl_sem,
    cond_send,
    cond_recv,
    msg_send,
    msg_recv,
    row_send,
    row_recv,
):
    faces, width = nu_ref.shape
    kinds = pat_ref.shape[0]
    rows = cw_ref.shape[1]
    me = lax.axis_index("dom")
    nxt = jnp.where(me == n - 1, 0, me + 1)
    prv = jnp.where(me == 0, n - 1, me - 1)

    def at(offset):
        target = me + offset
        return jnp.where(target >= n, target - n, target)

    barrier = pltpu.get_barrier_semaphore()

    def greet(offset, carry):
        pl.semaphore_signal(barrier, inc=1, device_id=(at(offset),), device_id_type=MESH)
        return carry

    lax.fori_loop(1, n, greet, 0)

    steps = faces // 8

    def curl_copy(step):
        part = pl.ds(step * 8, 8)
        return pltpu.make_async_copy(curl_hbm.at[:, part], curl.at[:, part], curl_sem.at[step])

    for step in range(steps):
        curl_copy(step).start()

    lane = row_iota(LANES)
    own_edge = (lane < 32) | (lane >= 96)
    low_edge = lane < 32
    high_edge = lane >= 96
    has_prev = me > 0
    has_next = me < n - 1
    halo_next = (lane >= 32) & (lane < 64) & has_next
    halo_prev = (lane >= 64) & (lane < 96) & has_prev
    halo_lanes = halo_next | halo_prev

    block_row = meta_ref[0:1, :].astype(jnp.int32)
    coil_row = meta_ref[1:2, :].astype(jnp.int32)
    inv_res = meta_ref[2:3, 0:LANES]
    source = meta_ref[3:4, 0:LANES]
    oh_blk[...] = onehot_of(block_row, LANES)
    oh_coil[...] = onehot_of(coil_row, LANES)

    def coil_rows(coil_values):
        wide = jnp.broadcast_to(coil_values, (16, LANES))
        high = wide.astype(BF16)
        rest = wide - high.astype(F32)
        mid = rest.astype(BF16)
        low = (rest - mid.astype(F32)).astype(BF16)
        parts = jnp.dot(
            jnp.concatenate([high, mid, low], axis=0), oh_coil[...], preferred_element_type=F32
        )
        return (parts[0:16] + parts[16:32] + parts[32:48])[0:1]

    def coupled(coil_values):
        return place(cw_ref[...] * coil_rows(coil_values), oh_blk[...])

    rhs = rs_ref[...] + coupled(source)

    coil_iota = lax.broadcasted_iota(jnp.int32, (LANES, LANES), 0)

    def tally(total, weighted, coils):
        for start in range(0, weighted.shape[1], LANES):
            part = weighted[:, start : start + LANES]
            named = coils[:, start : start + LANES]
            total = total + jnp.where(coil_iota == named, part, 0.0)
        return total

    def own_links(field):
        weighted = jnp.sum(cw_ref[...] * pick(field, oh_blk[...]), axis=0, keepdims=True)
        return tally(jnp.zeros((LANES, LANES), F32), weighted, coil_row)

    def as_row(total):
        return jnp.sum(total.T, axis=0, keepdims=True)

    msg[0] = jnp.where(own_edge, rhs, 0.0)
    row[0] = as_row(own_links(rhs))

    pl.semaphore_wait(barrier, n - 1)

    def sides(stage):
        return [
            pltpu.make_async_remote_copy(
                src_ref=msg.at[stage],
                dst_ref=msg_in.at[stage, side],
                send_sem=msg_send.at[stage, side],
                recv_sem=msg_recv.at[stage, side],
                device_id=(target,),
                device_id_type=MESH,
            )
            for side, target in ((0, nxt), (1, prv))
        ]

    def send(stage):
        for copy in sides(stage):
            copy.start()

        def one(offset, carry):
            pltpu.make_async_remote_copy(
                src_ref=row.at[stage],
                dst_ref=row_in.at[stage, offset - 1],
                send_sem=row_send.at[stage],
                recv_sem=row_recv.at[stage],
                device_id=(at(offset),),
                device_id_type=MESH,
            ).start()
            return carry

        lax.fori_loop(1, n, one, 0)

    def receive(stage):
        for copy in sides(stage):
            copy.wait()
        whole = row_in.at[stage]
        pltpu.make_async_copy(whole, whole, row_recv.at[stage]).wait()
        pltpu.make_async_copy(whole, whole, row_send.at[stage]).wait()
        from_prev = pltpu.roll(msg_in[stage, 0], LANES - 32, 1)
        from_next = pltpu.roll(msg_in[stage, 1], 32, 1)
        links = row[stage] + jnp.sum(row_in[stage], axis=0)
        return from_prev, from_next, links

    cond_copies = []
    for side, target in ((0, nxt), (1, prv)):
        for kind, (source_ref, dest_ref) in enumerate(((cw_ref, cw_nbr), (meta_ref, meta_nbr))):
            cond_copies.append(
                pltpu.make_async_remote_copy(
                    src_ref=source_ref,
                    dst_ref=dest_ref.at[side],
                    send_sem=cond_send.at[side, kind],
                    recv_sem=cond_recv.at[side, kind],
                    device_id=(target,),
                    device_id_type=MESH,
                )
            )

    send(0)
    for copy in cond_copies:
        copy.start()

    for k in range(kinds):
        named = pat_ref[k : k + 1, :]
        place_of = jnp.where(named < 32, named + 192, jnp.where(named < 160, named - 32, named))
        oh_pat[:, k * width : (k + 1) * width] = onehot_of(place_of, 2 * LANES)

    from_prev, from_next, links_r = receive(0)
    r = rhs
    r_halo = jnp.where(halo_next, from_next, jnp.where(halo_prev, from_prev, 0.0))
    x = jnp.zeros_like(r)
    p = s = s_halo = links_s = None
    rr_old = alpha = None

    for turn in range(ITERS):
        picked[...] = pick(jnp.concatenate([r, r_halo], axis=1), oh_pat[...])
        back[...] = jnp.zeros_like(back)
        dacc[...] = jnp.zeros_like(dacc)

        def faces_step(step, carry, turn=turn):
            if turn == 0:
                curl_copy(step).wait()
            start = pl.multiple_of(step * 8, 8)
            part = pl.ds(start, 8)
            flux = jnp.zeros((8, 8, width), F32)
            for k in range(kinds):
                for b in range(0, faces, 8):
                    seen = picked[b : b + 8, k * width : (k + 1) * width]
                    flux = flux + curl[k, part, b : b + 8, :] * seen[None]
            face = jnp.sum(flux, axis=1)
            weighted = nu_ref[part, :] * face
            dacc[...] += weighted * face
            wide = jnp.broadcast_to(weighted[:, None, :], (8, 8, width))
            for k in range(kinds):
                for b in range(0, faces, 8):
                    term = jnp.sum(curl[k, part, b : b + 8, :] * wide, axis=0)
                    back[b : b + 8, k * width : (k + 1) * width] += term
            return carry

        lax.fori_loop(0, steps, faces_step, 0)
        spread = place(back[...], oh_pat[...])
        spread_halo = jnp.where(halo_lanes, spread[:, LANES:], 0.0)
        sigma_r = sigma_ref[...] * r
        centre = sigma_r + spread[:, :LANES] + coupled(links_r * inv_res)
        msg[turn + 1] = jnp.where(own_edge, centre, spread_halo)
        rr_lanes = jnp.sum(r * r, axis=0, keepdims=True)
        rar_lanes = jnp.sum(sigma_r * r, axis=0, keepdims=True) + jnp.sum(
            dacc[...], axis=0, keepdims=True
        )
        if turn == 0:
            for copy in cond_copies:
                copy.wait()
            prev_block = meta_nbr[0, 0:1, :].astype(jnp.int32)
            next_block = meta_nbr[1, 0:1, :].astype(jnp.int32)
            prev_lane = jnp.where(prev_block >= 96, prev_block - 32, -1)
            next_lane = jnp.where(next_block < 32, next_block + 32, -1)
            oh_nbr[:, 0:rows] = onehot_of(prev_lane, LANES)
            oh_nbr[:, rows : 2 * rows] = onehot_of(next_lane, LANES)
        if turn + 1 < ITERS:
            total = own_links(centre)
            seen = pick(spread_halo, oh_nbr[...])
            for side in range(2):
                weighted = jnp.sum(
                    cw_nbr[side] * seen[:, side * rows : (side + 1) * rows], axis=0, keepdims=True
                )
                total = tally(total, weighted, meta_nbr[side, 1:2, :].astype(jnp.int32))
        else:
            total = jnp.zeros((LANES, LANES), F32)
        total = jnp.where(coil_iota == RR_ROW, rr_lanes, total)
        total = jnp.where(coil_iota == RAR_ROW, rar_lanes, total)
        row[turn + 1] = as_row(total)
        send(turn + 1)
        from_prev, from_next, links_q = receive(turn + 1)
        q = (
            centre
            + jnp.where(low_edge & has_prev, from_prev, 0.0)
            + jnp.where(high_edge & has_next, from_next, 0.0)
        )
        q_halo = spread_halo + jnp.where(
            halo_next, from_next, jnp.where(halo_prev, from_prev, 0.0)
        )
        rr = jnp.sum(jnp.where(lane == RR_ROW, links_q, 0.0), axis=1, keepdims=True)
        rar = jnp.sum(
            jnp.where(lane == RAR_ROW, links_q, links_r * links_r * inv_res),
            axis=1,
            keepdims=True,
        )
        if turn == 0:
            p, s, s_halo, links_s = r, q, q_halo, links_q
            alpha = rr / rar
        else:
            beta = rr / rr_old
            p = r + beta * p
            s = q + beta * s
            s_halo = q_halo + beta * s_halo
            links_s = links_q + beta * links_s
            alpha = rr / (rar - beta * rr / alpha)
        rr_old = rr
        x = x + alpha * p
        r = r - alpha * s
        r_halo = r_halo - alpha * s_halo
        links_r = links_r - alpha * links_s
    x_ref[...] = x
    r_ref[...] = r


def body(
    right_side,
    sigma,
    reluctivity,
    curl_blocks,
    pattern,
    cond_weight,
    cond_block,
    cond_coil,
    coil_phase,
    coil_resistance,
    switch_state,
):
    n = lax.axis_size("dom")
    width, count = right_side.shape
    kinds = pattern.shape[0]
    rows = cond_weight.shape[1]
    coils = coil_resistance.shape[0]
    states = switch_state.astype(F32)
    volts_of = states - jnp.mean(states)
    volts = jnp.zeros((coils,), F32)
    for phase in range(switch_state.shape[0]):
        volts = jnp.where(coil_phase == phase, LINK_SCALE * volts_of[phase], volts)
    pad = (0, rows - coils)
    meta = jnp.stack(
        [
            cond_block.astype(F32),
            cond_coil[:, 0].astype(F32),
            jnp.pad(1.0 / coil_resistance, pad),
            jnp.pad(volts / coil_resistance, pad),
        ]
        + [jnp.zeros((rows,), F32)] * 4
    )
    vmem = pl.BlockSpec(memory_space=pltpu.VMEM)
    stages = ITERS + 1
    shape = jax.ShapeDtypeStruct((width, count), F32)
    dma = pltpu.SemaphoreType.DMA
    return pl.pallas_call(
        functools.partial(kernel, n),
        out_shape=(shape, shape),
        in_specs=[vmem, vmem, vmem, pl.BlockSpec(memory_space=pl.ANY), vmem, vmem, vmem],
        out_specs=(vmem, vmem),
        scratch_shapes=[
            pltpu.VMEM(curl_blocks.shape, F32),
            pltpu.VMEM((2 * LANES, kinds * count), BF16),
            pltpu.VMEM((LANES, rows), BF16),
            pltpu.VMEM((LANES, 2 * rows), BF16),
            pltpu.VMEM((LANES, rows), BF16),
            pltpu.VMEM((width, kinds * count), F32),
            pltpu.VMEM((width, kinds * count), F32),
            pltpu.VMEM((8, count), F32),
            pltpu.VMEM((2, width, rows), F32),
            pltpu.VMEM((2, 8, rows), F32),
            pltpu.VMEM((stages, width, LANES), F32),
            pltpu.VMEM((stages, 2, width, LANES), F32),
            pltpu.VMEM((stages, 1, LANES), F32),
            pltpu.VMEM((stages, n - 1, 1, LANES), F32),
            dma((width // 8,)),
            dma((2, 2)),
            dma((2, 2)),
            dma((stages, 2)),
            dma((stages, 2)),
            dma((stages,)),
            dma((stages,)),
        ],
        compiler_params=pltpu.CompilerParams(
            collective_id=0, has_side_effects=True, vmem_limit_bytes=40 * 1024 * 1024
        ),
        cost_estimate=pl.CostEstimate(
            flops=4 * ITERS * curl_blocks.size, bytes_accessed=4 * curl_blocks.size, transcendentals=0
        ),
    )(right_side, sigma, reluctivity, curl_blocks, pattern, cond_weight, meta)


def solution(mesh):
    return jax.shard_map(
        body,
        mesh=mesh,
        in_specs=(
            P(None, "dom"),
            P(None, "dom"),
            P(None, "dom"),
            P(None, None, None, "dom"),
            P(None, "dom"),
            P(None, "dom"),
            P("dom"),
            P("dom", None),
            P(),
            P(),
            P(),
        ),
        out_specs=(P(None, "dom"), P(None, "dom")),
        check_vma=False,
    )
```

time: 490 us -> 52.2 us (0.11)
  blocking collectives: 344 us -> 0 us
  other arithmetic: 78 us -> 3.97 us
  Pallas kernels: 0 us -> 34 us
  starting transfers between devices: 32.8 us -> 0 us
  between operations: 8.6 us -> 3.3 us
  matrix products: 5.01 us -> 0 us
    psum x8 -> x0, blocking collectives: 344 us -> none  [the longest x3 132 us: body(): linkage = lax.psum(partial_link, 'dom')]
    pallas_call x0 -> x1, Pallas kernels: none -> 34 us  [body(): pl.pallas_call(functools.partial(kernel, n), out_shape=(shape, shape), in...]
    scatter-add x13 -> x0, other arithmetic: 33.8 us -> none  [the longest x3 18.2 us: body(): spread = jnp.zeros_like(extended).at[:, pattern].add(back_terms)]
    ppermute x12 -> x0, starting transfers between devices: 32.8 us -> none  [the longest x6 24 us: shifted(): return lax.ppermute(array, axis, pairs)]
    dot_general x3 -> x0, other arithmetic: 19.2 us -> none  [body(): jnp.einsum('kabn,bkn->an', curl_blocks, picked, precision=highest)]
    unnamed x9 -> x0, other arithmetic: 14.6 us -> none
    gather x6 -> x0, local copies, waits for them, and re-layouts: 7.83 us -> none  [the longest x3 4.72 us: body(): picked = jnp.take(extended, pattern, axis=1)]
    dot_general x8 -> x0, matrix products: 5.01 us -> none  [the longest x3 1.61 us: body(): jnp.dot(row_onehot, linkage / coil_resistance, precision=highest)]
  transfers between devices with their start and end apart: 12 -> 0, of which waited for: 3 -> 0; matrix products, arithmetic and copies ran while one was open for 2% -> 0% of each run, Pallas kernels for 0% -> 0%
where the time goes in v1:
time: 52.2 us; the launch traced here: 51.7 us
  Pallas kernels  34 us (65%)
  local copies, waits for them, and re-layouts  10.4 us (20%)
  other arithmetic  3.97 us (8%)
  between operations  3.3 us (6%)
    pallas_call x1, Pallas kernels, body(): pl.pallas_call(functools.partial(kernel, n), out_shape=(shape, shape), in...  34 us
    unnamed x14, local copies, waits for them, and re-layouts  9.66 us
    reduce_sum x1, other arithmetic, body(): volts_of = states - jnp.mean(states)  1.26 us

profile of v1, /device:TPU:0, one launch (start us, length us, event | category | flops | bytes accessed | tf_op | source)
XLA Modules:
  0.0 51.7 jit_solution(926899019438601366)
XLA Ops:
  0.6 1.3 %convert_reduce_fusion = f32[]{:T(128)} fusion(s32[3]{0:T(128)} %param.21), kind=kLoop, calls=%fused_computation.6 | loop fusion | flops 5 | bytes 16 | tf_op jit(solution)/shard_map/reduce_sum | solution.py:346
  2.5 0.7 %convert_subtract_fusion = f32[3]{0:T(128)S(1)} fusion(s32[3]{0:T(128)} %param.21, f32[]{:T(128)S(6)} %div.14), kind=kLoop, calls=%fused_computation.5 | loop fusion | flops 6 | bytes 28 | tf_op jit(solution)/shard_map/sub | solution.py:346
  3.2 0.7 %fusion.1 = (f32[1]{0:T(128)}, f32[1]{0:T(128)}, f32[1]{0:T(128)}) fusion(f32[3]{0:T(128)S(1)} %convert_subtract_fusion), kind=kLoop, calls=%fused_computation.8 | loop fusion | bytes 24 | tf_op jit(solution)/shard_map/slice | solution.py:349
  5.9 0.7 %fusion = (f32[84]{0:T(128)S(1)}, f32[84]{0:T(128)S(1)}) fusion(f32[84]{0:T(128)} %param.20, s32[84]{0:T(128)} %param.19, f32[]{:T(128)} %bitcast.5, f32[]{:T(128)} %bitcast.4, f32[]{:T(128)} %bitcast.3), kind=kLoop, calls=%fused_computation.4 | loop fusion | flops 672 | bytes 1356 | tf_op jit(solution)/shard_map/div | solution.py:356
  6.6 0.7 %convert_element_type.22 = f32[512]{0:T(512)S(1)} convert(s32[512]{0:T(512)} %param.17) | non-fusion elementwise | flops 512 | bytes 4096 | tf_op jit(solution)/shard_map/convert_element_type | solution.py:353
  7.2 0.7 %convert_bitcast_fusion = f32[1,512]{1,0:T(1,128)S(1)} fusion(s32[512,1]{0,1:T(1,128)} %param.18), kind=kLoop, calls=%fused_computation | loop fusion | flops 512 | bytes 4096 | tf_op jit(solution)/shard_map/convert_element_type | solution.py:354
  8.0 0.0 copy-start
  8.0 4.6 %copy-done = f32[6,64,64,128]{3,2,1,0:T(8,128)S(1)} copy-done((f32[6,64,64,128]{3,2,1,0:T(8,128)S(1)}, f32[6,64,64,128]{3,2,1,0:T(8,128)}, u32[]{:S(2)}) %copy-start) | copy-done | bytes 12582936
  12.5 0.0 copy-start.1
  12.5 0.9 %copy-done.1 = f32[64,512]{1,0:T(8,128)S(1)} copy-done((f32[64,512]{1,0:T(8,128)S(1)}, f32[64,512]{1,0:T(8,128)}, u32[]{:S(2)}) %copy-start.1) | copy-done | bytes 131096
  13.4 0.0 copy-start.2
  13.4 0.8 %copy-done.2 = f32[64,128]{1,0:T(8,128)S(1)} copy-done((f32[64,128]{1,0:T(8,128)S(1)}, f32[64,128]{1,0:T(8,128)}, u32[]{:S(2)}) %copy-start.2) | copy-done | bytes 32792
  14.2 0.0 copy-start.3
  14.2 0.8 %copy-done.3 = f32[64,128]{1,0:T(8,128)S(1)} copy-done((f32[64,128]{1,0:T(8,128)S(1)}, f32[64,128]{1,0:T(8,128)}, u32[]{:S(2)}) %copy-start.3) | copy-done | bytes 32792
  15.0 0.0 copy-start.4
  15.0 0.8 %copy-done.4 = f32[64,128]{1,0:T(8,128)S(1)} copy-done((f32[64,128]{1,0:T(8,128)S(1)}, f32[64,128]{1,0:T(8,128)}, u32[]{:S(2)}) %copy-start.4) | copy-done | bytes 32792
  15.7 0.0 copy-start.5
  15.7 0.7 %copy-done.5 = s32[6,128]{1,0:T(8,128)S(1)} copy-done((s32[6,128]{1,0:T(8,128)S(1)}, s32[6,128]{1,0:T(8,128)}, u32[]{:S(2)}) %copy-start.5) | copy-done | bytes 3096
  16.4 34.0 %shard_map.122 = (f32[64,128]{1,0:T(8,128)S(1)}, f32[64,128]{1,0:T(8,128)S(1)}) custom-call(f32[64,128]{1,0:T(8,128)S(1)} %copy-done.2, f32[64,128]{1,0:T(8,128)S(1)} %copy-done.3, f32[64,128]{1,0:T(8,128)S(1)} %copy-done.4, f32[6,64,64,128]{3,2,1,0:T(8,128)S(1)} %copy-done, s32[6,128]{1,0:T(8,128)S(1)} %copy-done.5, f32[64,512]{1,0:T(8,128)S(1)} %copy-done.1, ...), custom_call_target="tpu_custom_call" | custom-call | flops 37748736 | bytes 12582912 | tf_op jit(solution)/shard_map/pallas_call | solution.py:364
  50.4 0.6 %copy.15 = f32[64,128]{1,0:T(8,128)} copy(f32[64,128]{1,0:T(8,128)S(1)} %get-tuple-element.9) | data formatting | bytes 65536
  51.1 0.6 %copy.16 = f32[64,128]{1,0:T(8,128)} copy(f32[64,128]{1,0:T(8,128)S(1)} %get-tuple-element.10) | data formatting | bytes 65536
  (4 shorter events, 0.0 us)
Async XLA Ops:
  8.0 4.6 %copy-start = (f32[6,64,64,128]{3,2,1,0:T(8,128)S(1)}, f32[6,64,64,128]{3,2,1,0:T(8,128)}, u32[]{:S(2)}) copy-start(f32[6,64,64,128]{3,2,1,0:T(8,128)} %curl_hbm.1) | copy-start | bytes 37748740
  12.5 0.9 %copy-start.1 = (f32[64,512]{1,0:T(8,128)S(1)}, f32[64,512]{1,0:T(8,128)}, u32[]{:S(2)}) copy-start(f32[64,512]{1,0:T(8,128)} %cw_ref.1) | copy-start | bytes 393220
  13.4 0.8 %copy-start.2 = (f32[64,128]{1,0:T(8,128)S(1)}, f32[64,128]{1,0:T(8,128)}, u32[]{:S(2)}) copy-start(f32[64,128]{1,0:T(8,128)} %rs_ref.1) | copy-start | bytes 98308
  14.2 0.8 %copy-start.3 = (f32[64,128]{1,0:T(8,128)S(1)}, f32[64,128]{1,0:T(8,128)}, u32[]{:S(2)}) copy-start(f32[64,128]{1,0:T(8,128)} %sigma_ref.1) | copy-start | bytes 98308
  15.0 0.8 %copy-start.4 = (f32[64,128]{1,0:T(8,128)S(1)}, f32[64,128]{1,0:T(8,128)}, u32[]{:S(2)}) copy-start(f32[64,128]{1,0:T(8,128)} %nu_ref.1) | copy-start | bytes 98308
  15.7 0.7 %copy-start.5 = (s32[6,128]{1,0:T(8,128)S(1)}, s32[6,128]{1,0:T(8,128)}, u32[]{:S(2)}) copy-start(s32[6,128]{1,0:T(8,128)} %pat_ref.1) | copy-start | bytes 9220

commit v2 on v1

v2 whole, which is shorter than its diff:
```python
import functools

import jax
import jax.numpy as jnp
from jax import lax
from jax.experimental import pallas as pl
from jax.experimental.pallas import tpu as pltpu
from jax.sharding import PartitionSpec as P

ITERS = 3
LINK_SCALE = 16.0
LANES = 128
RR_ROW = 126
RAR_ROW = 127
MESH = pl.DeviceIdType.MESH
F32 = jnp.float32
BF16 = jnp.bfloat16


def split2(x):
    high = x.astype(BF16)
    low = (x - high.astype(F32)).astype(BF16)
    return jnp.concatenate([high, low], axis=0)


def pick(x, onehot):
    rows = x.shape[0]
    both = jnp.dot(split2(x), onehot, preferred_element_type=F32)
    return both[:rows] + both[rows:]


def place(x, onehot):
    rows = x.shape[0]
    both = lax.dot_general(
        split2(x), onehot, (((1,), (1,)), ((), ())), preferred_element_type=F32
    )
    return both[:rows] + both[rows:]


def onehot_of(index_row, height):
    iota = lax.broadcasted_iota(jnp.int32, (height, index_row.shape[1]), 0)
    return jnp.where(iota == index_row, 1.0, 0.0).astype(BF16)


def row_iota(width):
    return lax.broadcasted_iota(jnp.int32, (1, width), 1)


def kernel(
    n,
    rs_hbm,
    sigma_hbm,
    nu_hbm,
    curl_hbm,
    pat_hbm,
    cw_hbm,
    blk_hbm,
    coil_hbm,
    phase_hbm,
    res_hbm,
    state_hbm,
    out_ref,
    rs_ref,
    sigma_ref,
    nu_ref,
    pat_ref,
    cw_ref,
    blk_ref,
    coil_ref,
    phase_ref,
    res_ref,
    state_ref,
    curl,
    oh_pat,
    oh_blk,
    oh_nbr,
    oh_coil,
    picked,
    back,
    face_buf,
    coil_buf,
    cw_nbr,
    blk_nbr,
    coil_nbr,
    msg,
    msg_in,
    row,
    row_in,
    load_sem,
    curl_sem,
    cond_send,
    cond_recv,
    msg_send,
    msg_recv,
    row_send,
    row_recv,
):
    faces, width = nu_ref.shape
    kinds = pat_ref.shape[0]
    rows = cw_ref.shape[1]
    me = lax.axis_index("dom")
    nxt = jnp.where(me == n - 1, 0, me + 1)
    prv = jnp.where(me == 0, n - 1, me - 1)

    def at(offset):
        target = me + offset
        return jnp.where(target >= n, target - n, target)

    barrier = pltpu.get_barrier_semaphore()

    def greet(offset, carry):
        pl.semaphore_signal(barrier, inc=1, device_id=(at(offset),), device_id_type=MESH)
        return carry

    lax.fori_loop(1, n, greet, 0)

    steps = faces // 8

    def curl_copy(step):
        part = pl.ds(step * 8, 8)
        return pltpu.make_async_copy(curl_hbm.at[:, part], curl.at[:, part], curl_sem.at[step])

    loads = [
        pltpu.make_async_copy(source_ref, dest_ref, load_sem.at[i])
        for i, (source_ref, dest_ref) in enumerate(
            (
                (blk_hbm, blk_ref),
                (coil_hbm, coil_ref),
                (phase_hbm, phase_ref),
                (res_hbm, res_ref),
                (state_hbm, state_ref),
                (cw_hbm, cw_ref),
                (rs_hbm, rs_ref),
                (pat_hbm, pat_ref),
                (sigma_hbm, sigma_ref),
                (nu_hbm, nu_ref),
            )
        )
    ]
    for copy in loads:
        copy.start()
    for step in range(steps):
        curl_copy(step).start()
    coil_buf[...] = jnp.zeros_like(coil_buf)
    for copy in loads:
        copy.wait()

    lane = row_iota(LANES)
    own_edge = (lane < 32) | (lane >= 96)
    low_edge = lane < 32
    high_edge = lane >= 96
    has_prev = me > 0
    has_next = me < n - 1
    halo_next = (lane >= 32) & (lane < 64) & has_next
    halo_prev = (lane >= 64) & (lane < 96) & has_prev
    halo_lanes = halo_next | halo_prev

    block_row = blk_ref[...]
    coil_row = coil_ref[...]
    states = state_ref[...].astype(F32)
    phases = states.shape[1]
    centred = LINK_SCALE * (states - jnp.sum(states, axis=1, keepdims=True) / phases)
    volts = jnp.zeros(res_ref.shape, F32)
    for phase in range(phases):
        volts = jnp.where(phase_ref[...] == phase, centred[:, phase : phase + 1], volts)
    coils = res_ref.shape[1]
    coil_buf[0, :, 0:coils] = 1.0 / res_ref[...]
    coil_buf[1, :, 0:coils] = volts / res_ref[...]
    inv_res = coil_buf[0]
    source = coil_buf[1]
    oh_blk[...] = onehot_of(block_row, LANES)
    oh_coil[...] = onehot_of(coil_row, LANES)

    def coil_rows(coil_values):
        wide = jnp.broadcast_to(coil_values, (16, LANES))
        high = wide.astype(BF16)
        rest = wide - high.astype(F32)
        mid = rest.astype(BF16)
        low = (rest - mid.astype(F32)).astype(BF16)
        parts = jnp.dot(
            jnp.concatenate([high, mid, low], axis=0), oh_coil[...], preferred_element_type=F32
        )
        return (parts[0:16] + parts[16:32] + parts[32:48])[0:1]

    def coupled(coil_values):
        return place(cw_ref[...] * coil_rows(coil_values), oh_blk[...])

    rhs = rs_ref[...] + coupled(source)

    coil_iota = lax.broadcasted_iota(jnp.int32, (LANES, LANES), 0)

    def tally(total, weighted, coils):
        for start in range(0, weighted.shape[1], LANES):
            part = weighted[:, start : start + LANES]
            named = coils[:, start : start + LANES]
            total = total + jnp.where(coil_iota == named, part, 0.0)
        return total

    def own_links(field):
        weighted = jnp.sum(cw_ref[...] * pick(field, oh_blk[...]), axis=0, keepdims=True)
        return tally(jnp.zeros((LANES, LANES), F32), weighted, coil_row)

    def as_row(total):
        return jnp.sum(total.T, axis=0, keepdims=True)

    def sides(stage):
        return [
            pltpu.make_async_remote_copy(
                src_ref=msg.at[stage],
                dst_ref=msg_in.at[stage, side],
                send_sem=msg_send.at[stage, side],
                recv_sem=msg_recv.at[stage, side],
                device_id=(target,),
                device_id_type=MESH,
            )
            for side, target in ((0, nxt), (1, prv))
        ]

    def send_sides(stage):
        for copy in sides(stage):
            copy.start()

    def send_rows(stage):
        def one(offset, carry):
            pltpu.make_async_remote_copy(
                src_ref=row.at[stage],
                dst_ref=row_in.at[stage, offset - 1],
                send_sem=row_send.at[stage],
                recv_sem=row_recv.at[stage],
                device_id=(at(offset),),
                device_id_type=MESH,
            ).start()
            return carry

        lax.fori_loop(1, n, one, 0)

    def receive_sides(stage):
        for copy in sides(stage):
            copy.wait()
        return pltpu.roll(msg_in[stage, 0], LANES - 32, 1), pltpu.roll(msg_in[stage, 1], 32, 1)

    def receive_rows(stage):
        whole = row_in.at[stage]
        pltpu.make_async_copy(whole, whole, row_recv.at[stage]).wait()
        pltpu.make_async_copy(whole, whole, row_send.at[stage]).wait()
        return row[stage] + jnp.sum(row_in[stage], axis=0)

    def at_halo(from_prev, from_next):
        return jnp.where(halo_next, from_next, jnp.where(halo_prev, from_prev, 0.0))

    cond_copies = []
    for side, target in ((0, nxt), (1, prv)):
        for kind, (source_ref, dest_ref) in enumerate(
            ((cw_ref, cw_nbr), (blk_ref, blk_nbr), (coil_ref, coil_nbr))
        ):
            cond_copies.append(
                pltpu.make_async_remote_copy(
                    src_ref=source_ref,
                    dst_ref=dest_ref.at[side],
                    send_sem=cond_send.at[side, kind],
                    recv_sem=cond_recv.at[side, kind],
                    device_id=(target,),
                    device_id_type=MESH,
                )
            )

    def apply(field, halo, first):
        picked[...] = pick(jnp.concatenate([field, halo], axis=1), oh_pat[...])
        back[...] = jnp.zeros_like(back)

        def faces_step(step, carry):
            if first:
                curl_copy(step).wait()
            part = pl.ds(pl.multiple_of(step * 8, 8), 8)
            flux = jnp.zeros((8, 8, width), F32)
            for k in range(kinds):
                for b in range(0, faces, 8):
                    seen = picked[b : b + 8, k * width : (k + 1) * width]
                    flux = flux + curl[k, part, b : b + 8, :] * seen[None]
            face = jnp.sum(flux, axis=1)
            face_buf[part, :] = face
            weighted = nu_ref[part, :] * face
            wide = jnp.broadcast_to(weighted[:, None, :], (8, 8, width))
            for k in range(kinds):
                for b in range(0, faces, 8):
                    term = jnp.sum(curl[k, part, b : b + 8, :] * wide, axis=0)
                    back[b : b + 8, k * width : (k + 1) * width] += term
            return carry

        lax.fori_loop(0, steps, faces_step, 0)
        spread = place(back[...], oh_pat[...])
        return face_buf[...], spread[:, :LANES], jnp.where(halo_lanes, spread[:, LANES:], 0.0)

    msg[0] = jnp.where(own_edge, rhs, 0.0)
    pl.semaphore_wait(barrier, n - 1)
    send_sides(0)
    row[0] = as_row(own_links(rhs))
    send_rows(0)
    for copy in cond_copies:
        copy.start()
    for k in range(kinds):
        named = pat_ref[k : k + 1, :]
        place_of = jnp.where(named < 32, named + 192, jnp.where(named < 160, named - 32, named))
        oh_pat[:, k * width : (k + 1) * width] = onehot_of(place_of, 2 * LANES)

    r = rhs
    r_face, r_spread, r_spread_halo = apply(r, at_halo(*receive_sides(0)), True)
    links_r = receive_rows(0)
    x = jnp.zeros_like(r)

    for copy in cond_copies:
        copy.wait()
    prev_lane = jnp.where(blk_nbr[0] >= 96, blk_nbr[0] - 32, -1)
    next_lane = jnp.where(blk_nbr[1] < 32, blk_nbr[1] + 32, -1)
    oh_nbr[:, 0:rows] = onehot_of(prev_lane, LANES)
    oh_nbr[:, rows : 2 * rows] = onehot_of(next_lane, LANES)

    for turn in range(ITERS):
        last = turn + 1 == ITERS
        sigma_r = sigma_ref[...] * r
        rr_lanes = jnp.sum(r * r, axis=0, keepdims=True)
        rar_lanes = jnp.sum(sigma_r * r + nu_ref[...] * r_face * r_face, axis=0, keepdims=True)

        def send_total(total, turn=turn, rr_lanes=rr_lanes, rar_lanes=rar_lanes):
            total = jnp.where(coil_iota == RR_ROW, rr_lanes, total)
            total = jnp.where(coil_iota == RAR_ROW, rar_lanes, total)
            row[turn + 1] = as_row(total)
            send_rows(turn + 1)

        if last:
            send_total(jnp.zeros((LANES, LANES), F32))
        centre = sigma_r + r_spread + coupled(links_r * inv_res)
        msg[turn + 1] = jnp.where(own_edge, centre, r_spread_halo)
        send_sides(turn + 1)
        if not last:
            total = own_links(centre)
            seen = pick(r_spread_halo, oh_nbr[...])
            for side in range(2):
                weighted = jnp.sum(
                    cw_nbr[side] * seen[:, side * rows : (side + 1) * rows], axis=0, keepdims=True
                )
                total = tally(total, weighted, coil_nbr[side])
            send_total(total)
        from_prev, from_next = receive_sides(turn + 1)
        q = (
            centre
            + jnp.where(low_edge & has_prev, from_prev, 0.0)
            + jnp.where(high_edge & has_next, from_next, 0.0)
        )
        if not last:
            q_halo = r_spread_halo + at_halo(from_prev, from_next)
            q_face, q_spread, q_spread_halo = apply(q, q_halo, False)
        links_q = receive_rows(turn + 1)
        rr = jnp.sum(jnp.where(lane == RR_ROW, links_q, 0.0), axis=1, keepdims=True)
        rar = jnp.sum(
            jnp.where(lane == RAR_ROW, links_q, links_r * links_r * inv_res),
            axis=1,
            keepdims=True,
        )
        if turn == 0:
            p, s, links_s = r, q, links_q
            s_face, s_spread, s_spread_halo = q_face, q_spread, q_spread_halo
            alpha = rr / rar
        else:
            beta = rr / rr_old
            p = r + beta * p
            s = q + beta * s
            alpha = rr / (rar - beta * rr / alpha)
            if not last:
                links_s = links_q + beta * links_s
                s_face = q_face + beta * s_face
                s_spread = q_spread + beta * s_spread
                s_spread_halo = q_spread_halo + beta * s_spread_halo
        rr_old = rr
        x = x + alpha * p
        r = r - alpha * s
        if not last:
            links_r = links_r - alpha * links_s
            r_face = r_face - alpha * s_face
            r_spread = r_spread - alpha * s_spread
            r_spread_halo = r_spread_halo - alpha * s_spread_halo
    out_ref[0:faces, :] = x
    out_ref[faces : 2 * faces, :] = r


def body(
    right_side,
    sigma,
    reluctivity,
    curl_blocks,
    pattern,
    cond_weight,
    cond_block,
    cond_coil,
    coil_phase,
    coil_resistance,
    switch_state,
):
    n = lax.axis_size("dom")
    width, count = right_side.shape
    kinds = pattern.shape[0]
    rows = cond_weight.shape[1]
    vmem = pl.BlockSpec(memory_space=pltpu.VMEM)
    stages = ITERS + 1
    one_row = lambda array: array.reshape(1, -1)
    small = [one_row(array) for array in (cond_block, cond_coil, coil_phase, coil_resistance, switch_state)]
    arrays = [right_side, sigma, reluctivity, curl_blocks, pattern, cond_weight] + small
    loaded = [array for array in arrays if array is not curl_blocks]
    dma = pltpu.SemaphoreType.DMA
    out = pl.pallas_call(
        functools.partial(kernel, n),
        out_shape=jax.ShapeDtypeStruct((2 * width, count), F32),
        in_specs=[pl.BlockSpec(memory_space=pl.ANY)] * len(arrays),
        out_specs=vmem,
        scratch_shapes=[pltpu.VMEM(array.shape, array.dtype) for array in loaded]
        + [
            pltpu.VMEM(curl_blocks.shape, F32),
            pltpu.VMEM((2 * LANES, kinds * count), BF16),
            pltpu.VMEM((LANES, rows), BF16),
            pltpu.VMEM((LANES, 2 * rows), BF16),
            pltpu.VMEM((LANES, rows), BF16),
            pltpu.VMEM((width, kinds * count), F32),
            pltpu.VMEM((width, kinds * count), F32),
            pltpu.VMEM((width, count), F32),
            pltpu.VMEM((2, 1, LANES), F32),
            pltpu.VMEM((2, width, rows), F32),
            pltpu.VMEM((2, 1, rows), jnp.int32),
            pltpu.VMEM((2, 1, rows), jnp.int32),
            pltpu.VMEM((stages, width, LANES), F32),
            pltpu.VMEM((stages, 2, width, LANES), F32),
            pltpu.VMEM((stages, 1, LANES), F32),
            pltpu.VMEM((stages, n - 1, 1, LANES), F32),
            dma((len(loaded),)),
            dma((width // 8,)),
            dma((2, 3)),
            dma((2, 3)),
            dma((stages, 2)),
            dma((stages, 2)),
            dma((stages,)),
            dma((stages,)),
        ],
        compiler_params=pltpu.CompilerParams(
            collective_id=0, has_side_effects=True, vmem_limit_bytes=60 * 1024 * 1024
        ),
        cost_estimate=pl.CostEstimate(
            flops=4 * ITERS * curl_blocks.size, bytes_accessed=4 * curl_blocks.size, transcendentals=0
        ),
    )(*arrays)
    return out[:width], out[width:]


def solution(mesh):
    return jax.shard_map(
        body,
        mesh=mesh,
        in_specs=(
            P(None, "dom"),
            P(None, "dom"),
            P(None, "dom"),
            P(None, None, None, "dom"),
            P(None, "dom"),
            P(None, "dom"),
            P("dom"),
            P("dom", None),
            P(),
            P(),
            P(),
        ),
        out_specs=(P(None, "dom"), P(None, "dom")),
        check_vma=False,
    )
```

time: 52.2 us -> 37.5 us (0.72)
  local copies, waits for them, and re-layouts: 10.4 us -> 1.4 us
  other arithmetic: 3.97 us -> 0 us
  between operations: 3.3 us -> 0.64 us
  Pallas kernels: 34 us -> 35.3 us
    unnamed x14 -> x0, local copies, waits for them, and re-layouts: 9.66 us -> none
    convert_element_type x2 -> x0, other arithmetic: 1.37 us -> none  [the longest x1 0.69 us: body(): cond_block.astype(F32)]
    reduce_sum x1 -> x0, other arithmetic: 1.26 us -> none  [body(): volts_of = states - jnp.mean(states)]
    pallas_call x1, Pallas kernels: 34 us -> 35.3 us  [body(): pl.pallas_call(functools.partial(kernel, n), out_shape=jax.ShapeDtypeStru...]
    slice x1, local copies, waits for them, and re-layouts: 0.67 us -> 1.4 us  [body(): return (out[:width], out[width:])]
    div x1 -> x0, other arithmetic: 0.68 us -> none  [body(): volts / coil_resistance]
    sub x1 -> x0, other arithmetic: 0.66 us -> none  [body(): volts_of = states - jnp.mean(states)]
where the time goes in v2:
time: 37.5 us; the launch traced here: 37.3 us
  Pallas kernels  35.3 us (94%)
  local copies, waits for them, and re-layouts  1.4 us (4%)
  between operations  0.64 us (2%)
    pallas_call x1, Pallas kernels, body(): pl.pallas_call(functools.partial(kernel, n), out_shape=jax.ShapeDtypeStru...  35.3 us
    slice x1, local copies, waits for them, and re-layouts, body(): return (out[:width], out[width:])  1.4 us

profile of v2, /device:TPU:0, one launch (start us, length us, event | category | flops | bytes accessed | tf_op | source)
XLA Modules:
  0.0 37.3 jit_solution(5398791979404029550)
XLA Ops:
  0.6 35.3 %shard_map.122 = f32[128,128]{1,0:T(8,128)} custom-call(f32[64,128]{1,0:T(8,128)} %rs_hbm.1, f32[64,128]{1,0:T(8,128)} %sigma_hbm.1, f32[64,128]{1,0:T(8,128)} %nu_hbm.1, f32[6,64,64,128]{3,2,1,0:T(8,128)} %curl_hbm.1, s32[6,128]{1,0:T(8,128)} %pat_hbm.1, f32[64,512]{1,0:T(8,128)} %cw_hbm.1, s32[1,512]{1,0:T(1,128)} %bitcast.5, s32[1,512]{1,0:T(1,128)} %bitcast.6, ...), custom_call_target="tpu_custom_call" | custom-call | flops 37748736 | bytes 12582912 | tf_op jit(solution)/shard_map/pallas_call | solution.py:410
  35.9 1.4 %fusion = (f32[64,128]{1,0:T(8,128)}, f32[64,128]{1,0:T(8,128)}) fusion(f32[128,128]{1,0:T(8,128)} %shard_map.122), kind=kLoop, calls=%fused_computation | loop fusion | bytes 131072 | tf_op jit(solution)/shard_map/slice | solution.py:449

commit v3 on v2

--- a/solution.py
+++ b/solution.py
@@ -10,6 +10,7 @@
 ITERS = 3
 LINK_SCALE = 16.0
 LANES = 128
+STEP = 16
 RR_ROW = 126
 RAR_ROW = 127
 MESH = pl.DeviceIdType.MESH
@@ -29,17 +30,14 @@
     return both[:rows] + both[rows:]
 
 
-def place(x, onehot):
-    rows = x.shape[0]
-    both = lax.dot_general(
-        split2(x), onehot, (((1,), (1,)), ((), ())), preferred_element_type=F32
-    )
-    return both[:rows] + both[rows:]
-
-
 def onehot_of(index_row, height):
     iota = lax.broadcasted_iota(jnp.int32, (height, index_row.shape[1]), 0)
     return jnp.where(iota == index_row, 1.0, 0.0).astype(BF16)
+
+
+def onehot_across(index_column, width):
+    iota = lax.broadcasted_iota(jnp.int32, (index_column.shape[0], width), 1).astype(F32)
+    return jnp.where(iota == index_column, 1.0, 0.0).astype(BF16)
 
 
 def row_iota(width):
@@ -72,7 +70,9 @@
     state_ref,
     curl,
     oh_pat,
+    oh_pat_t,
     oh_blk,
+    oh_blk_t,
     oh_nbr,
     oh_coil,
     picked,
@@ -169,6 +169,8 @@
     inv_res = coil_buf[0]
     source = coil_buf[1]
     oh_blk[...] = onehot_of(block_row, LANES)
+    block_column = jnp.broadcast_to(block_row, (8, rows)).astype(F32).T
+    oh_blk_t[...] = onehot_across(block_column[:, 0:1], LANES)
     oh_coil[...] = onehot_of(coil_row, LANES)
 
     def coil_rows(coil_values):
@@ -183,7 +185,7 @@
         return (parts[0:16] + parts[16:32] + parts[32:48])[0:1]
 
     def coupled(coil_values):
-        return place(cw_ref[...] * coil_rows(coil_values), oh_blk[...])
+        return pick(cw_ref[...] * coil_rows(coil_values), oh_blk_t[...])
 
     rhs = rs_ref[...] + coupled(source)
 
@@ -232,7 +234,11 @@
             ).start()
             return carry
 
-        lax.fori_loop(1, n, one, 0)
+        if n <= 32:
+            for offset in range(1, n):
+                one(offset, 0)
+        else:
+            lax.fori_loop(1, n, one, 0)
 
     def receive_sides(stage):
         for copy in sides(stage):
@@ -270,9 +276,10 @@
 
         def faces_step(step, carry):
             if first:
-                curl_copy(step).wait()
-            part = pl.ds(pl.multiple_of(step * 8, 8), 8)
-            flux = jnp.zeros((8, 8, width), F32)
+                for half in range(STEP // 8):
+                    curl_copy(step * (STEP // 8) + half).wait()
+            part = pl.ds(pl.multiple_of(step * STEP, STEP), STEP)
+            flux = jnp.zeros((STEP, 8, width), F32)
             for k in range(kinds):
                 for b in range(0, faces, 8):
                     seen = picked[b : b + 8, k * width : (k + 1) * width]
@@ -280,15 +287,15 @@
             face = jnp.sum(flux, axis=1)
             face_buf[part, :] = face
             weighted = nu_ref[part, :] * face
-            wide = jnp.broadcast_to(weighted[:, None, :], (8, 8, width))
+            wide = jnp.broadcast_to(weighted[:, None, :], (STEP, 8, width))
             for k in range(kinds):
                 for b in range(0, faces, 8):
                     term = jnp.sum(curl[k, part, b : b + 8, :] * wide, axis=0)
                     back[b : b + 8, k * width : (k + 1) * width] += term
             return carry
 
-        lax.fori_loop(0, steps, faces_step, 0)
-        spread = place(back[...], oh_pat[...])
+        lax.fori_loop(0, faces // STEP, faces_step, 0)
+        spread = pick(back[...], oh_pat_t[...])
         return face_buf[...], spread[:, :LANES], jnp.where(halo_lanes, spread[:, LANES:], 0.0)
 
     msg[0] = jnp.where(own_edge, rhs, 0.0)
@@ -298,10 +305,14 @@
     send_rows(0)
     for copy in cond_copies:
         copy.start()
+    named = pat_ref[...]
+    place_of = jnp.where(named < 32, named + 192, jnp.where(named < 160, named - 32, named))
+    spare = jnp.zeros((8 - kinds % 8, width), jnp.int32)
+    place_column = jnp.concatenate([place_of, spare], axis=0).astype(F32).T
     for k in range(kinds):
-        named = pat_ref[k : k + 1, :]
-        place_of = jnp.where(named < 32, named + 192, jnp.where(named < 160, named - 32, named))
-        oh_pat[:, k * width : (k + 1) * width] = onehot_of(place_of, 2 * LANES)
+        part = slice(k * width, (k + 1) * width)
+        oh_pat[:, part] = onehot_of(place_of[k : k + 1, :], 2 * LANES)
+        oh_pat_t[part, :] = onehot_across(place_column[:, k : k + 1], 2 * LANES)
 
     r = rhs
     r_face, r_spread, r_spread_halo = apply(r, at_halo(*receive_sides(0)), True)
@@ -416,7 +427,9 @@
         + [
             pltpu.VMEM(curl_blocks.shape, F32),
             pltpu.VMEM((2 * LANES, kinds * count), BF16),
+            pltpu.VMEM((kinds * count, 2 * LANES), BF16),
             pltpu.VMEM((LANES, rows), BF16),
+            pltpu.VMEM((rows, LANES), BF16),
             pltpu.VMEM((LANES, 2 * rows), BF16),
             pltpu.VMEM((LANES, rows), BF16),
             pltpu.VMEM((width, kinds * count), F32),

time: 37.5 us -> 36.5 us (0.973)
  Pallas kernels: 35.3 us -> 34.2 us
    pallas_call x1, Pallas kernels: 35.3 us -> 34.2 us  [body(): pl.pallas_call(functools.partial(kernel, n), out_shape=jax.ShapeDtypeStru...]
where the time goes in v3:
time: 36.5 us; the launch traced here: 36.3 us
  Pallas kernels  34.2 us (94%)
  local copies, waits for them, and re-layouts  1.4 us (4%)
  between operations  0.64 us (2%)
    pallas_call x1, Pallas kernels, body(): pl.pallas_call(functools.partial(kernel, n), out_shape=jax.ShapeDtypeStru...  34.2 us
    slice x1, local copies, waits for them, and re-layouts, body(): return (out[:width], out[width:])  1.4 us

profile of v3, /device:TPU:0, one launch (start us, length us, event | category | flops | bytes accessed | tf_op | source)
XLA Modules:
  0.0 36.3 jit_solution(16192693872314553524)
XLA Ops:
  0.6 34.2 %shard_map.122 = f32[128,128]{1,0:T(8,128)} custom-call(f32[64,128]{1,0:T(8,128)} %rs_hbm.1, f32[64,128]{1,0:T(8,128)} %sigma_hbm.1, f32[64,128]{1,0:T(8,128)} %nu_hbm.1, f32[6,64,64,128]{3,2,1,0:T(8,128)} %curl_hbm.1, s32[6,128]{1,0:T(8,128)} %pat_hbm.1, f32[64,512]{1,0:T(8,128)} %cw_hbm.1, s32[1,512]{1,0:T(1,128)} %bitcast.5, s32[1,512]{1,0:T(1,128)} %bitcast.6, ...), custom_call_target="tpu_custom_call" | custom-call | flops 37748736 | bytes 12582912 | tf_op jit(solution)/shard_map/pallas_call | solution.py:421
  34.9 1.4 %fusion = (f32[64,128]{1,0:T(8,128)}, f32[64,128]{1,0:T(8,128)}) fusion(f32[128,128]{1,0:T(8,128)} %shard_map.122), kind=kLoop, calls=%fused_computation | loop fusion | bytes 131072 | tf_op jit(solution)/shard_map/slice | solution.py:462

commit v4 on v3

--- a/solution.py
+++ b/solution.py
@@ -155,6 +155,19 @@
     halo_prev = (lane >= 64) & (lane < 96) & has_prev
     halo_lanes = halo_next | halo_prev
 
+    departs = (has_next, has_prev)
+    arrives = (has_prev, has_next)
+
+    def clear(side):
+        for stage in range(ITERS + 1):
+            msg_in[stage, side] = jnp.zeros(msg_in.shape[2:], F32)
+        cw_nbr[side] = jnp.zeros(cw_nbr.shape[1:], F32)
+        blk_nbr[side] = jnp.zeros(blk_nbr.shape[1:], jnp.int32)
+        coil_nbr[side] = jnp.zeros(coil_nbr.shape[1:], jnp.int32)
+
+    for side in range(2):
+        pl.when(jnp.logical_not(arrives[side]))(functools.partial(clear, side))
+
     block_row = blk_ref[...]
     coil_row = coil_ref[...]
     states = state_ref[...].astype(F32)
@@ -219,8 +232,8 @@
         ]
 
     def send_sides(stage):
-        for copy in sides(stage):
-            copy.start()
+        for side, copy in enumerate(sides(stage)):
+            pl.when(departs[side])(copy.start)
 
     def send_rows(stage):
         def one(offset, carry):
@@ -241,14 +254,13 @@
             lax.fori_loop(1, n, one, 0)
 
     def receive_sides(stage):
-        for copy in sides(stage):
-            copy.wait()
+        for side, copy in enumerate(sides(stage)):
+            pl.when(arrives[side])(copy.wait_recv)
         return pltpu.roll(msg_in[stage, 0], LANES - 32, 1), pltpu.roll(msg_in[stage, 1], 32, 1)
 
     def receive_rows(stage):
         whole = row_in.at[stage]
         pltpu.make_async_copy(whole, whole, row_recv.at[stage]).wait()
-        pltpu.make_async_copy(whole, whole, row_send.at[stage]).wait()
         return row[stage] + jnp.sum(row_in[stage], axis=0)
 
     def at_halo(from_prev, from_next):
@@ -259,7 +271,7 @@
         for kind, (source_ref, dest_ref) in enumerate(
             ((cw_ref, cw_nbr), (blk_ref, blk_nbr), (coil_ref, coil_nbr))
         ):
-            cond_copies.append(
+            cond_copies.append((side,
                 pltpu.make_async_remote_copy(
                     src_ref=source_ref,
                     dst_ref=dest_ref.at[side],
@@ -267,7 +279,7 @@
                     recv_sem=cond_recv.at[side, kind],
                     device_id=(target,),
                     device_id_type=MESH,
-                )
+                ))
             )
 
     def apply(field, halo, first):
@@ -295,6 +307,8 @@
             return carry
 
         lax.fori_loop(0, faces // STEP, faces_step, 0)
+
+    def gathered():
         spread = pick(back[...], oh_pat_t[...])
         return face_buf[...], spread[:, :LANES], jnp.where(halo_lanes, spread[:, LANES:], 0.0)
 
@@ -303,8 +317,8 @@
     send_sides(0)
     row[0] = as_row(own_links(rhs))
     send_rows(0)
-    for copy in cond_copies:
-        copy.start()
+    for side, copy in cond_copies:
+        pl.when(departs[side])(copy.start)
     named = pat_ref[...]
     place_of = jnp.where(named < 32, named + 192, jnp.where(named < 160, named - 32, named))
     spare = jnp.zeros((8 - kinds % 8, width), jnp.int32)
@@ -315,12 +329,13 @@
         oh_pat_t[part, :] = onehot_across(place_column[:, k : k + 1], 2 * LANES)
 
     r = rhs
-    r_face, r_spread, r_spread_halo = apply(r, at_halo(*receive_sides(0)), True)
+    apply(r, at_halo(*receive_sides(0)), True)
+    for side, copy in cond_copies:
+        pl.when(arrives[side])(copy.wait_recv)
     links_r = receive_rows(0)
+    r_face, r_spread, r_spread_halo = gathered()
     x = jnp.zeros_like(r)
 
-    for copy in cond_copies:
-        copy.wait()
     prev_lane = jnp.where(blk_nbr[0] >= 96, blk_nbr[0] - 32, -1)
     next_lane = jnp.where(blk_nbr[1] < 32, blk_nbr[1] + 32, -1)
     oh_nbr[:, 0:rows] = onehot_of(prev_lane, LANES)
@@ -360,8 +375,10 @@
         )
         if not last:
             q_halo = r_spread_halo + at_halo(from_prev, from_next)
-            q_face, q_spread, q_spread_halo = apply(q, q_halo, False)
+            apply(q, q_halo, False)
         links_q = receive_rows(turn + 1)
+        if not last:
+            q_face, q_spread, q_spread_halo = gathered()
         rr = jnp.sum(jnp.where(lane == RR_ROW, links_q, 0.0), axis=1, keepdims=True)
         rar = jnp.sum(
             jnp.where(lane == RAR_ROW, links_q, links_r * links_r * inv_res),
@@ -392,6 +409,13 @@
             r_spread_halo = r_spread_halo - alpha * s_spread_halo
     out_ref[0:faces, :] = x
     out_ref[faces : 2 * faces, :] = r
+    for side, copy in cond_copies:
+        pl.when(departs[side])(copy.wait_send)
+    for stage in range(ITERS + 1):
+        for side, copy in enumerate(sides(stage)):
+            pl.when(departs[side])(copy.wait_send)
+        whole = row_in.at[stage]
+        pltpu.make_async_copy(whole, whole, row_send.at[stage]).wait()
 
 
 def body(

time: 36.5 us -> 33.6 us (0.921)
  Pallas kernels: 34.2 us -> 31.4 us
    pallas_call x1, Pallas kernels: 34.2 us -> 31.4 us  [body(): pl.pallas_call(functools.partial(kernel, n), out_shape=jax.ShapeDtypeStru...]
where the time goes in v4:
time: 33.6 us; the launch traced here: 33.4 us
  Pallas kernels  31.4 us (93%)
  local copies, waits for them, and re-layouts  1.4 us (4%)
  between operations  0.64 us (2%)
    pallas_call x1, Pallas kernels, body(): pl.pallas_call(functools.partial(kernel, n), out_shape=jax.ShapeDtypeStru...  31.4 us
    slice x1, local copies, waits for them, and re-layouts, body(): return (out[:width], out[width:])  1.4 us

profile of v4, /device:TPU:0, one launch (start us, length us, event | category | flops | bytes accessed | tf_op | source)
XLA Modules:
  0.0 33.4 jit_solution(5487630647867925630)
XLA Ops:
  0.6 31.4 %shard_map.122 = f32[128,128]{1,0:T(8,128)} custom-call(f32[64,128]{1,0:T(8,128)} %rs_hbm.1, f32[64,128]{1,0:T(8,128)} %sigma_hbm.1, f32[64,128]{1,0:T(8,128)} %nu_hbm.1, f32[6,64,64,128]{3,2,1,0:T(8,128)} %curl_hbm.1, s32[6,128]{1,0:T(8,128)} %pat_hbm.1, f32[64,512]{1,0:T(8,128)} %cw_hbm.1, s32[1,512]{1,0:T(1,128)} %bitcast.5, s32[1,512]{1,0:T(1,128)} %bitcast.6, ...), custom_call_target="tpu_custom_call" | custom-call | flops 37748736 | bytes 12582912 | tf_op jit(solution)/shard_map/pallas_call | solution.py:445
  32.0 1.4 %fusion = (f32[64,128]{1,0:T(8,128)}, f32[64,128]{1,0:T(8,128)}) fusion(f32[128,128]{1,0:T(8,128)} %shard_map.122), kind=kLoop, calls=%fused_computation | loop fusion | bytes 131072 | tf_op jit(solution)/shard_map/slice | solution.py:486
